TPU v7x, 128 devices: a whole 4x4x4 slice. The times are simulated.
128 devices in a mesh: grp: 16 (over y_lo, z, core), tp: 8 (over x, y_hi).
Axes of the slice: x: 4, y: 4 (y_hi: 2, y_lo: 2; y = y_hi * 2 + y_lo), z: 4, core: 2. Of those that a mesh axis runs over, the one named last changes fastest.
Arguments:
- tokens: bfloat16 [2, 5120, 4096], P(None, 'grp', 'tp'), may hold values from -6 to 6
- norm_gain: float32 [4096], replicated, may hold values from 0.5 to 1.5
- up_master: float32 [4096, 16384], P(('grp', 'tp')), may hold values from -6 to 6
- up_gradient: bfloat16 [4096, 16384], P(('grp', 'tp')), may hold values from -0.59765625 to 0.59765625
- up_first: float32 [4096, 16384], P(('grp', 'tp')), may hold values from -0.18 to 0.18
- up_second: float32 [4096, 16384], P(('grp', 'tp')), may hold values from 0.0001 to 0.01
- down_master: float32 [16384, 4096], P(('grp', 'tp')), may hold values from -6 to 6
- down_gradient: bfloat16 [16384, 4096], P(('grp', 'tp')), may hold values from -0.59765625 to 0.59765625
- down_first: float32 [16384, 4096], P(('grp', 'tp')), may hold values from -0.18 to 0.18
- down_second: float32 [16384, 4096], P(('grp', 'tp')), may hold values from 0.0001 to 0.01
Outputs:
- up_updated: float32 [4096, 16384], P(('grp', 'tp'))
- down_updated: float32 [16384, 4096], P(('grp', 'tp'))
- decoded: bfloat16 [2, 5120, 4096], P(None, 'grp', 'tp')
All inputs are finite; a program needn't handle non-finite values.
Results may differ from a plain program's by a relative error of at most 0.015.
Values may be sent and summed in bfloat16 or wider, within the bound.
No kernel may reach another device: no remote copies, remote signals or barrier semaphores. Data moves between devices by JAX's collectives and lax.ppermute only.
A program may use at most 192 MiB of HBM per device.

v0:
```python
import jax
import jax.numpy as jnp
from jax import lax
from jax.sharding import PartitionSpec as P

learn_rate = 0.05
beta_one = 0.9
beta_two = 0.95
adam_eps = 1e-08
decay_rate = 0.1
step_index = 100
norm_eps = 1e-06


def adamw_update(master, gradient, first_moment, second_moment):
    grad_float = gradient.astype(jnp.float32)
    first_new = beta_one * first_moment + (1.0 - beta_one) * grad_float
    second_new = beta_two * second_moment + (1.0 - beta_two) * grad_float * grad_float
    corr_one = 1.0 - beta_one**step_index
    corr_two = 1.0 - beta_two**step_index
    update = first_new / corr_one / (jnp.sqrt(second_new / corr_two) + adam_eps)
    return master - learn_rate * (update + decay_rate * master)


def body(
    tokens,
    norm_gain,
    up_master,
    up_gradient,
    up_first,
    up_second,
    down_master,
    down_gradient,
    down_first,
    down_second,
):
    up_updated = adamw_update(up_master, up_gradient, up_first, up_second)
    down_updated = adamw_update(down_master, down_gradient, down_first, down_second)
    group_count = lax.axis_size("grp")
    shard_count = lax.axis_size("tp")
    up_rows, hidden_width = up_updated.shape
    block_width = hidden_width // (group_count * shard_count)
    model_width = up_rows * group_count * shard_count
    up_cast = up_updated.astype(jnp.bfloat16).reshape(
        up_rows, group_count, shard_count, block_width
    )
    down_cast = down_updated.astype(jnp.bfloat16)
    owned = lax.all_to_all(up_cast, "tp", split_axis=2, concat_axis=0, tiled=True)
    up_local = lax.all_gather(owned, "grp", axis=0, tiled=True).reshape(
        model_width, group_count * block_width
    )
    features_all = lax.all_gather(tokens, "tp", axis=2, tiled=True)
    step_count, row_count, _ = features_all.shape
    flat_rows = features_all.reshape(step_count * row_count, model_width).astype(jnp.float32)
    mean_sq = jnp.mean(flat_rows * flat_rows, axis=-1, keepdims=True)
    normed = (flat_rows * lax.rsqrt(mean_sq + norm_eps) * norm_gain).astype(jnp.bfloat16)
    hidden = jax.nn.silu(
        jnp.dot(normed, up_local, preferred_element_type=jnp.float32) * model_width ** (-0.5)
    ).astype(jnp.bfloat16)
    down_local = lax.all_gather(down_cast, "grp", axis=0, tiled=True)
    running = jnp.dot(hidden, down_local, preferred_element_type=jnp.float32)
    partial_term = running * hidden_width ** (-0.5)
    summed = lax.psum_scatter(
        partial_term.astype(jnp.bfloat16), "tp", scatter_dimension=1, tiled=True
    )
    decoded = summed.reshape(step_count, row_count, model_width // shard_count)
    return (up_updated, down_updated, decoded)


def solution(mesh):
    in_specs = (
        P(None, "grp", "tp"),
        P(),
        P(("grp", "tp"), None),
        P(("grp", "tp"), None),
        P(("grp", "tp"), None),
        P(("grp", "tp"), None),
        P(("grp", "tp"), None),
        P(("grp", "tp"), None),
        P(("grp", "tp"), None),
        P(("grp", "tp"), None),
    )
    out_specs = (P(("grp", "tp"), None), P(("grp", "tp"), None), P(None, "grp", "tp"))
    return jax.shard_map(body, mesh=mesh, in_specs=in_specs, out_specs=out_specs, check_vma=False)
```

profile of v0, /device:TPU:1, one launch (start us, length us, event | category | flops | bytes accessed | tf_op | source)
XLA Modules:
  0.0 412.3 jit_solution(1639237604253128803)
XLA Ops:
  7.2 0.0 all-gather.4.cloned.1.call-start
  7.2 0.7 all-gather.4.cloned.1.call-update
  7.9 0.0 all-gather.6.cloned.1.call-start
  7.9 6.2 %convert_bitcast_fusion = (bf16[4,8,128,128]{3,1,2,0:T(8,128)(2,1)S(1)}, f32[32,16384]{1,0:T(8,128)}) fusion(f32[32,16384]{1,0:T(8,128)} %param.12, f32[32,16384]{1,0:T(8,128)} %param.15, bf16[32,16384]{1,0:T(8,128)(2,1)} %param.13, f32[32,16384]{1,0:T(8,128)} %param.14), kind=kLoop, calls=%fused_computation.33 | loop fusion | flops 8912896 | bytes 10485760
  14.1 0.2 copy.19
  14.4 0.1 copy.16
  14.5 0.0 copy-start.1
  14.5 0.0 copy-start.2
  14.6 26.2 %all_to_all.18 = bf16[32,16,8,128]{3,1,0,2:T(8,128)(2,1)} all-to-all(bf16[32,16,8,128]{3,1,0,2:T(8,128)(2,1)S(1)} %copy.16), channel_id=1, replica_groups=mesh['grp'=16,'tp'=8] {'tp'}, dimensions={2} | all-to-all | bytes 2097152 | tf_op jit(solution)/shard_map/all_to_all | solution.py:48
  40.8 0.0 all-gather.6.cloned.1.call-update
  40.8 0.0 all-gather.8.cloned.1.call-start
  40.8 0.0 copy-done.1
  40.9 0.0 copy-done.2
  40.9 5.5 %fusion.28 = (bf16[128,4096]{1,0:T(8,128)(2,1)}, f32[128,4096]{1,0:T(8,128)}) fusion(f32[128,4096]{1,0:T(8,128)S(1)} %copy-done.1, f32[128,4096]{1,0:T(8,128)} %param.19, bf16[128,4096]{1,0:T(8,128)(2,1)S(1)} %copy-done.2, f32[128,4096]{1,0:T(8,128)} %param.18), kind=kLoop, calls=%fused_computation.37 | loop fusion | flops 8912896 | bytes 10485760 | tf_op jit(solution)/shard_map/convert_element_type | solution.py:47
  46.4 0.0 copy-start.3
  46.4 0.0 all-gather.8.cloned.1.call-update
  46.4 0.0 reduce-scatter.2.cloned.1.call-start
  46.5 63.5 %all-gather.4.cloned.1.call-done = bf16[2,320,4096]{2,1,0:T(8,128)(2,1)} async-done(((bf16[2,320,512]{2,1,0:T(8,128)(2,1)}), bf16[2,320,4096]{2,1,0:T(8,128)(2,1)}) %all-gather.4.cloned.1.call-update) | async-done | bytes 5242896 | tf_op jit(solution)/shard_map/all_gather | solution.py:52
  109.9 0.0 copy-start
  109.9 3.7 fusion
  113.7 0.0 copy-done.3
  113.7 0.3 copy-done
  114.0 4.5 %fusion.2 = bf16[2,320,4096]{2,1,0:T(8,128)(2,1)} fusion(bf16[2,320,4096]{2,1,0:T(8,128)(2,1)S(1)} %copy-done, f32[4096]{0:T(1024)S(1)} %copy-done.3, f32[2,320]{1,0:T(2,128)S(1)} %add_rsqrt_fusion), kind=kLoop, calls=%fused_computation.4 | loop fusion | flops 10485760 | bytes 10504704 | tf_op jit(solution)/shard_map/convert_element_type | solution.py:56
  118.5 85.0 %all-gather.6.cloned.1.call-done = bf16[4096,16,1,128]{3,1,2,0:T(8,128)(2,1)} async-done(((bf16[256,16,1,128]{3,1,2,0:T(8,128)(2,1)}), bf16[4096,16,1,128]{3,1,2,0:T(8,128)(2,1)}) %all-gather.6.cloned.1.call-update) | async-done | bytes 16777232 | tf_op jit(solution)/shard_map/all_gather | solution.py:49
  203.5 22.2 %copy.18 = bf16[4096,16,1,128]{0,3,1,2:T(8,128)(2,1)} copy(bf16[4096,16,1,128]{3,1,2,0:T(8,128)(2,1)} %all-gather.6.cloned.1.call-done) | data formatting | bytes 33554432 | tf_op jit(solution)/shard_map/all_gather | solution.py:49
  225.7 17.1 %multiply_convert_fusion.1.clone.4 = bf16[640,2048]{1,0:T(8,128)(2,1)S(1)} fusion(bf16[640,4096]{1,0:T(8,128)(2,1)} %bitcast.26, bf16[4096,2048]{0,1:T(8,128)(2,1)} %bitcast.25), kind=kOutput, calls=%fused_computation.6.clone.clone.clone.1 | convolution fusion | flops 10745282560 | bytes 24641536 | tf_op jit(solution)/shard_map/dot_general | solution.py:58
  242.8 55.1 %all-gather.8.cloned.1.call-done = bf16[2048,4096]{1,0:T(8,128)(2,1)} async-done(((bf16[128,4096]{1,0:T(8,128)(2,1)}), bf16[2048,4096]{1,0:T(8,128)(2,1)}) %all-gather.8.cloned.1.call-update) | async-done | bytes 16777232 | tf_op jit(solution)/shard_map/all_gather | solution.py:60
  297.8 16.1 %multiply_convert_fusion = bf16[640,4096]{1,0:T(8,128)(2,1)} fusion(bf16[2048,4096]{1,0:T(8,128)(2,1)} %all-gather.8.cloned.1.call-done, bf16[640,2048]{1,0:T(8,128)(2,1)S(1)} %multiply_convert_fusion.1.clone.4), kind=kOutput, calls=%fused_computation.5 | convolution fusion | flops 10742661120 | bytes 24641536 | tf_op jit(solution)/shard_map/dot_general | solution.py:61
  314.0 0.0 reduce-scatter.2.cloned.1.call-update
  314.0 91.7 %reduce-scatter.2.cloned.1.call-done = bf16[640,512]{1,0:T(8,128)(2,1)} async-done(((bf16[640,4096]{1,0:T(8,128)(2,1)}), bf16[640,512]{1,0:T(8,128)(2,1)}) %reduce-scatter.2.cloned.1.call-update) | async-done | bytes 655376 | tf_op jit(solution)/shard_map/reduce_scatter | solution.py:63
  (1 shorter events, 0.0 us)
Async XLA Ops:
  7.2 102.8 %all-gather.4.cloned.1.call-start = ((), (), s32[]{:S(2)}) async-start(), calls=%async_computation.2 | async-start | bytes 5898240 | tf_op jit(solution)/shard_map/all_gather | solution.py:52
  7.9 195.6 %all-gather.6.cloned.1.call-start = ((), (), s32[]{:S(2)}) async-start(), calls=%async_computation.3 | async-start | bytes 17825792 | tf_op jit(solution)/shard_map/all_gather | solution.py:49
  14.5 26.3 %copy-start.1 = (f32[128,4096]{1,0:T(8,128)S(1)}, f32[128,4096]{1,0:T(8,128)}, u32[]{:S(2)}) copy-start(f32[128,4096]{1,0:T(8,128)} %param.16) | copy-start | bytes 6291460
  14.5 26.3 %copy-start.2 = (bf16[128,4096]{1,0:T(8,128)(2,1)S(1)}, bf16[128,4096]{1,0:T(8,128)(2,1)}, u32[]{:S(2)}) copy-start(bf16[128,4096]{1,0:T(8,128)(2,1)} %param.17) | copy-start | bytes 3145732
  40.8 257.0 %all-gather.8.cloned.1.call-start = ((), (), s32[]{:S(2)}) async-start(), calls=%async_computation.4 | async-start | bytes 17825792 | tf_op jit(solution)/shard_map/all_gather | solution.py:60
  46.4 67.3 %copy-start.3 = (f32[4096]{0:T(1024)S(1)}, f32[4096]{0:T(1024)}, u32[]{:S(2)}) copy-start(f32[4096]{0:T(1024)} %param.11) | copy-start | bytes 49156
  46.4 359.3 %reduce-scatter.2.cloned.1.call-start = ((), (), s32[]{:S(2)}) async-start(), calls=%async_computation.5 | async-start | bytes 5898240 | tf_op jit(solution)/shard_map/reduce_scatter | solution.py:63
  109.9 4.0 copy-start
Sparse Core Ops, SparseCore 0:
  10.2 99.6 all-gather.3
  111.6 91.7 all-gather.5
  205.2 92.6 all-gather.7
  314.1 91.5 reduce-scatter.1
where the time goes:
time: 413 us; the launch traced here: 412 us
  waiting for transfers between devices  296 us (72%)
  matrix products  33.2 us (8%)
  blocking collectives  26.2 us (6%)
  local copies, waits for them, and re-layouts  22.9 us (6%)
  other arithmetic  20 us (5%)
  between operations  13.8 us (3%)
    reduce_scatter x1, waiting for transfers between devices, body(): lax.psum_scatter(partial_term.astype(jnp.bfloat16), 'tp', scatter_dimensi...  91.7 us
    all_gather x1, waiting for transfers between devices, body(): lax.all_gather(owned, 'grp', axis=0, tiled=True)  85 us
    all_gather x1, waiting for transfers between devices, body(): features_all = lax.all_gather(tokens, 'tp', axis=2, tiled=True)  63.5 us
    all_gather x1, waiting for transfers between devices, body(): down_local = lax.all_gather(down_cast, 'grp', axis=0, tiled=True)  55.1 us
    all_to_all x1, blocking collectives, body(): lax.all_to_all(up_cast, 'tp', split_axis=2, concat_axis=0, tiled=True)  26.2 us
    all_gather x1, local copies, waits for them, and re-layouts, body(): lax.all_gather(owned, 'grp', axis=0, tiled=True)  22.2 us
    dot_general x1, matrix products, body(): jnp.dot(normed, up_local, preferred_element_type=jnp.float32)  17.1 us
    dot_general x1, matrix products, body(): running = jnp.dot(hidden, down_local, preferred_element_type=jnp.float32)  16.1 us
  transfers between devices with their start and end apart: 4, of which 4 were waited for; matrix products, arithmetic and copies ran while one was open for 14% of the time, Pallas kernels for 0%

commit v1 on v0

--- a/solution.py
+++ b/solution.py
@@ -10,6 +10,13 @@
 decay_rate = 0.1
 step_index = 100
 norm_eps = 1e-06
+
+
+def gather_over(x, mesh_axis, dim):
+    count = lax.axis_size(mesh_axis)
+    blocks = jnp.stack([x for _ in range(count)])
+    blocks = lax.all_to_all(blocks, mesh_axis, split_axis=0, concat_axis=0)
+    return jnp.concatenate(blocks, axis=dim)
 
 
 def adamw_update(master, gradient, first_moment, second_moment):
@@ -49,7 +56,7 @@
     up_local = lax.all_gather(owned, "grp", axis=0, tiled=True).reshape(
         model_width, group_count * block_width
     )
-    features_all = lax.all_gather(tokens, "tp", axis=2, tiled=True)
+    features_all = gather_over(tokens, "tp", 2)
     step_count, row_count, _ = features_all.shape
     flat_rows = features_all.reshape(step_count * row_count, model_width).astype(jnp.float32)
     mean_sq = jnp.mean(flat_rows * flat_rows, axis=-1, keepdims=True)

time: 413 us -> 395 us (0.956)
  waiting for transfers between devices: 296 us -> 264 us
  local copies, waits for them, and re-layouts: 22.9 us -> 35.3 us
  starting transfers between devices: 0.16 us -> 5.09 us
    all_to_all x0 -> x1, waiting for transfers between devices: none -> 73.5 us  [gather_over(): blocks = lax.all_to_all(blocks, mesh_axis, split_axis=0, concat_axis=0)]
    all_gather x1 -> x0, waiting for transfers between devices: 63.5 us -> none  [body(): features_all = lax.all_gather(tokens, 'tp', axis=2, tiled=True)]
    all_gather x1, waiting for transfers between devices: 85 us -> 43.9 us  [body(): lax.all_gather(owned, 'grp', axis=0, tiled=True)]
    unnamed x9 -> x8, local copies, waits for them, and re-layouts: 0.54 us -> 6.1 us
    all_to_all x0 -> x1, starting transfers between devices: none -> 4.79 us  [gather_over(): blocks = lax.all_to_all(blocks, mesh_axis, split_axis=0, concat_axis=0)]
  transfers between devices with their start and end apart: 4 -> 4, of which waited for: 4 -> 4; matrix products, arithmetic and copies ran while one was open for 14% -> 17% of each run, Pallas kernels for 0% -> 0%
where the time goes in v1:
time: 395 us; the launch traced here: 394 us
  waiting for transfers between devices  264 us (67%)
  local copies, waits for them, and re-layouts  35.3 us (9%)
  matrix products  33.2 us (8%)
  blocking collectives  22.9 us (6%)
  other arithmetic  19.6 us (5%)
  between operations  13.8 us (3%)
  starting transfers between devices  5.09 us (1%)
    reduce_scatter x1, waiting for transfers between devices, body(): lax.psum_scatter(partial_term.astype(jnp.bfloat16), 'tp', scatter_dimensi...  91.8 us
    all_to_all x1, waiting for transfers between devices, gather_over(): blocks = lax.all_to_all(blocks, mesh_axis, split_axis=0, concat_axis=0)  73.5 us
    all_gather x1, waiting for transfers between devices, body(): down_local = lax.all_gather(down_cast, 'grp', axis=0, tiled=True)  55.1 us
    all_gather x1, waiting for transfers between devices, body(): lax.all_gather(owned, 'grp', axis=0, tiled=True)  43.9 us
    all_to_all x1, blocking collectives, body(): lax.all_to_all(up_cast, 'tp', split_axis=2, concat_axis=0, tiled=True)  22.9 us
    all_gather x1, local copies, waits for them, and re-layouts, body(): lax.all_gather(owned, 'grp', axis=0, tiled=True)  22.2 us
    dot_general x1, matrix products, body(): jnp.dot(normed, up_local, preferred_element_type=jnp.float32)  17.1 us
    dot_general x1, matrix products, body(): running = jnp.dot(hidden, down_local, preferred_element_type=jnp.float32)  16.1 us
  transfers between devices with their start and end apart: 4, of which 4 were waited for; matrix products, arithmetic and copies ran while one was open for 17% of the time, Pallas kernels for 0%

profile of v1, /device:TPU:1, one launch (start us, length us, event | category | flops | bytes accessed | tf_op | source)
XLA Modules:
  0.0 394.2 jit_solution(8594701417283608860)
XLA Ops:
  7.2 0.0 all-gather.3.cloned.1.call-start
  7.2 6.2 %convert_bitcast_fusion = (bf16[4,8,128,128]{3,1,2,0:T(8,128)(2,1)S(1)}, f32[32,16384]{1,0:T(8,128)}) fusion(f32[32,16384]{1,0:T(8,128)} %param.12, f32[32,16384]{1,0:T(8,128)} %param.15, bf16[32,16384]{1,0:T(8,128)(2,1)} %param.13, f32[32,16384]{1,0:T(8,128)} %param.14), kind=kLoop, calls=%fused_computation.34 | loop fusion | flops 8912896 | bytes 10485760
  13.4 0.2 copy.21
  13.6 0.1 copy.17
  13.8 0.0 copy-start
  13.8 0.0 copy-start.1
  13.8 22.9 %all_to_all.23 = bf16[32,16,8,128]{3,1,0,2:T(8,128)(2,1)} all-to-all(bf16[32,16,8,128]{3,1,0,2:T(8,128)(2,1)S(1)} %copy.17), channel_id=1, replica_groups=mesh['grp'=16,'tp'=8] {'tp'}, dimensions={2} | all-to-all | bytes 2097152 | tf_op jit(solution)/shard_map/all_to_all | solution.py:55
  36.7 0.0 all-gather.3.cloned.1.call-update
  36.7 0.0 all-gather.5.cloned.1.call-start
  36.8 0.0 copy-done
  36.8 0.0 copy-done.1
  36.8 5.5 %fusion.29 = (bf16[128,4096]{1,0:T(8,128)(2,1)}, f32[128,4096]{1,0:T(8,128)}) fusion(f32[128,4096]{1,0:T(8,128)S(1)} %copy-done, f32[128,4096]{1,0:T(8,128)} %param.19, bf16[128,4096]{1,0:T(8,128)(2,1)S(1)} %copy-done.1, f32[128,4096]{1,0:T(8,128)} %param.18), kind=kLoop, calls=%fused_computation.38 | loop fusion | flops 8912896 | bytes 10485760 | tf_op jit(solution)/shard_map/convert_element_type | solution.py:54
  42.3 0.0 all-gather.5.cloned.1.call-update
  42.4 3.9 stack.2
  46.3 0.0 copy-start.2
  46.3 4.8 %all-to-all-start = ((bf16[8,2,320,512]{3,2,1,0:T(8,128)(2,1)}), bf16[8,2,320,512]{3,2,1,0:T(8,128)(2,1)}, u32[]{:S(2)}, u32[]{:S(2)}) async-start(bf16[8,2,320,512]{3,2,1,0:T(8,128)(2,1)} %stack.2), calls=%async_computation | async-start | bytes 10485760 | tf_op jit(solution)/shard_map/all_to_all | solution.py:18
  51.1 0.2 reduce-scatter.2.cloned.1.call-start
  51.3 0.0 copy-done.2
  51.3 73.5 %all-to-all-done = bf16[8,2,320,512]{3,2,1,0:T(8,128)(2,1)} async-done(((bf16[8,2,320,512]{3,2,1,0:T(8,128)(2,1)}), bf16[8,2,320,512]{3,2,1,0:T(8,128)(2,1)}, u32[]{:S(2)}, u32[]{:S(2)}) %all-to-all-start) | async-done | bytes 5242912 | tf_op jit(solution)/shard_map/all_to_all | solution.py:18
  124.8 3.7 fusion
  128.6 4.1 %fusion.3 = bf16[2,320,8,512]{3,1,0,2:T(8,128)(2,1)S(1)} fusion(bf16[8,2,320,512]{3,2,1,0:T(8,128)(2,1)} %all-to-all-done, f32[8,512]{1,0:T(8,128)S(1)} %mul.118, f32[2,320]{1,0:T(2,128)S(1)} %add_rsqrt_fusion), kind=kLoop, calls=%fused_computation.6 | loop fusion | flops 10485760 | bytes 10504704 | tf_op jit(solution)/shard_map/convert_element_type | solution.py:63
  132.7 3.0 copy.16
  135.6 5.8 %copy.20 = bf16[80,8,8,512]{3,1,2,0:T(8,128)(2,1)} copy(bf16[80,8,8,512]{3,2,1,0:T(8,128)(2,1)S(1)} %bitcast.29) | data formatting | bytes 10485760
  141.5 43.9 %all-gather.3.cloned.1.call-done = bf16[4096,16,1,128]{3,1,2,0:T(8,128)(2,1)} async-done(((bf16[256,16,1,128]{3,1,2,0:T(8,128)(2,1)}), bf16[4096,16,1,128]{3,1,2,0:T(8,128)(2,1)}) %all-gather.3.cloned.1.call-update) | async-done | bytes 16777232 | tf_op jit(solution)/shard_map/all_gather | solution.py:56
  185.4 22.2 %copy.19 = bf16[4096,16,1,128]{0,3,1,2:T(8,128)(2,1)} copy(bf16[4096,16,1,128]{3,1,2,0:T(8,128)(2,1)} %all-gather.3.cloned.1.call-done) | data formatting | bytes 33554432 | tf_op jit(solution)/shard_map/all_gather | solution.py:56
  207.6 17.1 %multiply_convert_fusion.1.clone.4 = bf16[640,2048]{1,0:T(8,128)(2,1)S(1)} fusion(bf16[640,4096]{1,0:T(8,128)(2,1)} %bitcast.31, bf16[4096,2048]{0,1:T(8,128)(2,1)} %bitcast.30), kind=kOutput, calls=%fused_computation.7.clone.clone.clone.1 | convolution fusion | flops 10745282560 | bytes 24641536 | tf_op jit(solution)/shard_map/dot_general | solution.py:65
  224.7 55.1 %all-gather.5.cloned.1.call-done = bf16[2048,4096]{1,0:T(8,128)(2,1)} async-done(((bf16[128,4096]{1,0:T(8,128)(2,1)}), bf16[2048,4096]{1,0:T(8,128)(2,1)}) %all-gather.5.cloned.1.call-update) | async-done | bytes 16777232 | tf_op jit(solution)/shard_map/all_gather | solution.py:67
  279.8 16.1 %multiply_convert_fusion = bf16[640,4096]{1,0:T(8,128)(2,1)} fusion(bf16[2048,4096]{1,0:T(8,128)(2,1)} %all-gather.5.cloned.1.call-done, bf16[640,2048]{1,0:T(8,128)(2,1)S(1)} %multiply_convert_fusion.1.clone.4), kind=kOutput, calls=%fused_computation.5 | convolution fusion | flops 10742661120 | bytes 24641536 | tf_op jit(solution)/shard_map/dot_general | solution.py:68
  295.9 0.0 reduce-scatter.2.cloned.1.call-update
  295.9 91.8 %reduce-scatter.2.cloned.1.call-done = bf16[640,512]{1,0:T(8,128)(2,1)} async-done(((bf16[640,4096]{1,0:T(8,128)(2,1)}), bf16[640,512]{1,0:T(8,128)(2,1)}) %reduce-scatter.2.cloned.1.call-update) | async-done | bytes 655376 | tf_op jit(solution)/shard_map/reduce_scatter | solution.py:70
  (2 shorter events, 0.0 us)
Async XLA Ops:
  7.2 178.3 %all-gather.3.cloned.1.call-start = ((), (), s32[]{:S(2)}) async-start(), calls=%async_computation.3 | async-start | bytes 17825792 | tf_op jit(solution)/shard_map/all_gather | solution.py:56
  13.8 23.0 %copy-start = (f32[128,4096]{1,0:T(8,128)S(1)}, f32[128,4096]{1,0:T(8,128)}, u32[]{:S(2)}) copy-start(f32[128,4096]{1,0:T(8,128)} %param.16) | copy-start | bytes 6291460
  13.8 23.0 %copy-start.1 = (bf16[128,4096]{1,0:T(8,128)(2,1)S(1)}, bf16[128,4096]{1,0:T(8,128)(2,1)}, u32[]{:S(2)}) copy-start(bf16[128,4096]{1,0:T(8,128)(2,1)} %param.17) | copy-start | bytes 3145732
  36.7 243.0 %all-gather.5.cloned.1.call-start = ((), (), s32[]{:S(2)}) async-start(), calls=%async_computation.4 | async-start | bytes 17825792 | tf_op jit(solution)/shard_map/all_gather | solution.py:67
  46.3 5.0 %copy-start.2 = (f32[4096]{0:T(1024)S(1)}, f32[4096]{0:T(1024)}, u32[]{:S(2)}) copy-start(f32[4096]{0:T(1024)} %param.11) | copy-start | bytes 49156
  46.3 78.5 %all-to-all-start = ((bf16[8,2,320,512]{3,2,1,0:T(8,128)(2,1)}), bf16[8,2,320,512]{3,2,1,0:T(8,128)(2,1)}, u32[]{:S(2)}, u32[]{:S(2)}) async-start(bf16[8,2,320,512]{3,2,1,0:T(8,128)(2,1)} %stack.2), calls=%async_computation | async-start | bytes 10485760 | tf_op jit(solution)/shard_map/all_to_all | solution.py:18
  51.1 336.6 %reduce-scatter.2.cloned.1.call-start = ((), (), s32[]{:S(2)}) async-start(), calls=%async_computation.5 | async-start | bytes 5898240 | tf_op jit(solution)/shard_map/reduce_scatter | solution.py:70
Sparse Core Ops, SparseCore 0:
  36.9 148.5 all-gather.2
  187.1 92.5 all-gather.4
  296.0 91.6 reduce-scatter.1
